TPU v7x, 32 devices: a whole 2x2x4 slice. The times are simulated.
32 devices in a mesh: dp: 2 (over y), ctx: 16 (over z, x, core).
Axes of the slice: x: 2, y: 2, z: 4, core: 2. Of those that a mesh axis runs over, the one named last changes fastest.
Arguments:
- query_in: bfloat16 [2, 2048, 1792], P('dp', 'ctx'), may hold values from -8 to 8
- key_in: bfloat16 [2, 2048, 256], P('dp', 'ctx'), may hold values from -4 to 4
- value_input: bfloat16 [2, 2048, 256], P('dp', 'ctx'), may hold values from -4 to 4
- output_gradient: bfloat16 [2, 2048, 1792], P('dp', 'ctx'), may hold values from -5 to 5
- doc_ids: int32 [2, 2048], P('dp', 'ctx'), may hold values from 0 to 1, as said below
- query_bias: float32 [1792], replicated, may hold values from -2 to 2
Outputs:
- attended: bfloat16 [2, 2048, 1792], P('dp', 'ctx')
- grad_query: bfloat16 [2, 2048, 1792], P('dp', 'ctx')
- key_gradient: bfloat16 [2, 2048, 256], P('dp', 'ctx')
- value_gradient: bfloat16 [2, 2048, 256], P('dp', 'ctx')
- grad_bias: float32 [1792], replicated
Inputs may be any that keep to these rules, and one draw needn't show every extreme that they name: `doc_ids`: ids never fall along a sequence; each of the 2 documents of a sequence holds 512 to 1536 tokens, and together they fill all 2048 tokens.
All inputs are finite; a program needn't handle non-finite values.
Results may differ from a plain program's by a relative error of at most 0.019.
Values may be sent and summed in bfloat16 or wider, within the bound.
No kernel may reach another device: no remote copies, remote signals or barrier semaphores. Data moves between devices by JAX's collectives and lax.ppermute only.
A program may use at most 64 MiB of HBM per device.

v0:
```python
import functools
import math

import jax
import jax.numpy as jnp
from jax import lax
from jax.experimental import pallas as pl
from jax.experimental.pallas import tpu as pltpu
from jax.sharding import PartitionSpec as P

QUERY_HEADS = 14
KEY_VALUE_HEADS = 2
HEAD_SIZE = 128
GROUP_SIZE = 7
BLK = 128
WB = 16
DOC_ROWS = 16
PAIR = 4
LEVEL = 4
LANE_TILE = 256
KV_WIDTH = 2 * KEY_VALUE_HEADS * HEAD_SIZE
SCALE = 1.0 / math.sqrt(HEAD_SIZE)
SCALE_LOG2 = SCALE * math.log2(math.e)
LOW = -1e30

NT = (((1,), (1,)), ((), ()))


def fold(value, op):
    keys, lanes = value.shape
    return op(value.reshape(keys // 8, 8, lanes), axis=0)


def window_levels(shards):
    levels = max(shards // LEVEL, 1)
    return min((WB - 2 + LEVEL) // LEVEL, max(3 * levels // 4 - 1, 0) if levels % 4 == 0 else levels - 1)


def pack_kernel(key_hbm, value_hbm, docs_hbm, own_ref, docs, sems):
    rows, half = key_hbm.shape
    copies = [
        pltpu.make_async_copy(docs_hbm, docs, sems.at[0]),
        pltpu.make_async_copy(key_hbm, own_ref.at[0:rows, 0:half], sems.at[1]),
        pltpu.make_async_copy(value_hbm, own_ref.at[0:rows, half:2 * half], sems.at[2]),
    ]
    for copy in copies:
        copy.start()
    copies[0].wait()
    count = jnp.sum((docs[...] == 0).astype(jnp.float32), axis=1, keepdims=True)
    own_ref[rows:rows + DOC_ROWS, :] = jnp.broadcast_to(count, (DOC_ROWS, 2 * half)).astype(
        jnp.bfloat16
    )
    copies[1].wait()
    copies[2].wait()


def pack(key_in, value_input, doc_ids):
    rows, half = key_in.shape
    return pl.pallas_call(
        pack_kernel,
        out_shape=jax.ShapeDtypeStruct((rows + DOC_ROWS, 2 * half), jnp.bfloat16),
        in_specs=[pl.BlockSpec(memory_space=pltpu.HBM)] * 3,
        out_specs=pl.BlockSpec(memory_space=pltpu.VMEM),
        scratch_shapes=[pltpu.VMEM((1, rows), jnp.int32), pltpu.SemaphoreType.DMA((3,))],
        compiler_params=pltpu.CompilerParams(vmem_limit_bytes=60 * 1024 * 1024),
        name="pack",
    )(key_in, value_input, doc_ids)


def head_columns(g, n):
    head = g * GROUP_SIZE + n
    return slice(head * HEAD_SIZE, (head + 1) * HEAD_SIZE)


def prepare_kernel(q_hbm, bias_ref, do_hbm, own_hbm, q_st, do_t, own_ref, q_buf, do_buf, sems):
    rows = q_buf.shape[0]
    first = pltpu.make_async_copy(q_hbm, q_buf, sems.at[0])
    second = pltpu.make_async_copy(do_hbm, do_buf, sems.at[1])
    third = pltpu.make_async_copy(own_hbm, own_ref, sems.at[2])
    first.start()
    second.start()
    third.start()
    first.wait()
    for g in range(KEY_VALUE_HEADS):
        for n in range(GROUP_SIZE):
            columns = head_columns(g, n)
            q_st[g, n * rows:(n + 1) * rows, :] = (
                q_buf[:, columns].astype(jnp.float32) + bias_ref[:, columns]
            ).astype(jnp.bfloat16)
    second.wait()
    for g in range(KEY_VALUE_HEADS):
        for n in range(GROUP_SIZE):
            do_t[g, :, n * rows:(n + 1) * rows] = do_buf[:, head_columns(g, n)].T
    third.wait()


def prepare(query_in, query_bias, output_gradient, own):
    rows, width = query_in.shape
    lanes = GROUP_SIZE * rows
    anywhere = pl.BlockSpec(memory_space=pltpu.HBM)
    vmem = pl.BlockSpec(memory_space=pltpu.VMEM)
    return pl.pallas_call(
        prepare_kernel,
        out_shape=(
            jax.ShapeDtypeStruct((KEY_VALUE_HEADS, lanes, HEAD_SIZE), jnp.bfloat16),
            jax.ShapeDtypeStruct((KEY_VALUE_HEADS, HEAD_SIZE, lanes), jnp.bfloat16),
            jax.ShapeDtypeStruct(own.shape, own.dtype),
        ),
        in_specs=[anywhere, vmem, anywhere, anywhere],
        out_specs=(vmem, vmem, vmem),
        scratch_shapes=[
            pltpu.VMEM((rows, width), jnp.bfloat16),
            pltpu.VMEM((rows, width), jnp.bfloat16),
            pltpu.SemaphoreType.DMA((3,)),
        ],
        compiler_params=pltpu.CompilerParams(vmem_limit_bytes=8 * 1024 * 1024),
        cost_estimate=pl.CostEstimate(
            flops=4 * rows * width, bytes_accessed=8 * rows * width, transcendentals=0
        ),
        name="prepare",
    )(query_in, query_bias, output_gradient, own)


def keys_of(kv_buf, c, rows, column):
    columns = slice(column * HEAD_SIZE, (column + 1) * HEAD_SIZE)
    return jnp.concatenate([kv_buf[PAIR * c + i, 0:rows, columns] for i in range(PAIR)], axis=0)


def spread(kv_buf, slot, pieces, inner):
    core = inner % 2
    x = inner // 2
    for at, piece in enumerate(pieces):
        place_x = 1 - x if at % 2 else x
        place_core = 1 - core if at // 2 else core
        kv_buf[slot * LEVEL + 2 * place_x + place_core] = piece[...]


def doc_count(kv_buf, rows):
    counts = kv_buf[:, rows:rows + DOC_ROWS, 0:128].astype(jnp.float32)
    return jnp.sum(counts) * (1.0 / (DOC_ROWS * 128))


def window_start(rank, rows, first, count):
    boundary = (count + 0.5).astype(jnp.int32) + jnp.maximum(first, 0) * rows
    low_block = jnp.maximum(rank - (WB - 1), 0)
    in_second = rank * rows >= boundary
    return boundary, jnp.where(in_second, jnp.maximum(low_block, boundary // rows), low_block)


def mask_bias(key_first, q_first, boundary, chunk, rows):
    key_pos = key_first + lax.broadcasted_iota(jnp.int32, (chunk, rows), 0)
    query_pos = q_first + lax.broadcasted_iota(jnp.int32, (chunk, rows), 1)
    allowed = (key_pos <= query_pos) & (query_pos // BLK - key_pos // BLK < WB)
    allowed = allowed & ((key_pos >= boundary) == (query_pos >= boundary))
    return jnp.where(allowed, 0.0, LOW)


def lane_tiles(lanes):
    return [(at, min(at + LANE_TILE, lanes)) for at in range(0, lanes, LANE_TILE)]


def near_kernel(
    rank_ref, q_all, near_ref, near_core_ref,
    kv_buf, p_buf, stats_ref, acc,
    s_buf,
):
    packed = kv_buf.shape[1]
    depth, chunk = p_buf.shape[:2]
    rows = chunk // PAIR
    lanes = q_all.shape[1]
    tiles = lane_tiles(lanes)
    rank = rank_ref[0]
    first = (rank // LEVEL - (depth - 1)) * LEVEL
    for level in range(depth):
        pieces = [
            ref.at[at * packed:(at + 1) * packed]
            for ref in (near_ref, near_core_ref) for at in (2 * level, 2 * level + 1)
        ]
        spread(kv_buf, depth - 1 - level, pieces, rank % LEVEL)
    boundary, low_block = window_start(rank, rows, first, doc_count(kv_buf, rows))
    low = jnp.maximum(low_block - first, 0) // PAIR

    for g in range(KEY_VALUE_HEADS):
        stats_ref[g, 0:8, :] = jnp.full((8, lanes), LOW, jnp.float32)
        stats_ref[g, 8:16, :] = jnp.zeros((8, lanes), jnp.float32)
    acc[...] = jnp.zeros_like(acc)

    def score_steps(c, g):
        bias = mask_bias((first + PAIR * c) * rows, rank * rows, boundary, chunk, rows)
        k_c = keys_of(kv_buf, c, rows, g)

        def step(a, b):
            s = lax.dot_general(k_c, q_all[g, a:b, :], NT, preferred_element_type=jnp.float32)
            s = s + jnp.concatenate([bias] * ((b - a) // rows), axis=1)
            s_buf[c, :, a:b] = s
            stats_ref[g, 0:8, a:b] = jnp.maximum(stats_ref[g, 0:8, a:b], fold(s, jnp.max))

        return step

    def weight_steps(c, g, row_max):
        v_t = keys_of(kv_buf, c, rows, KEY_VALUE_HEADS + g).T

        def step(a, b):
            p = jnp.exp2(s_buf[c, :, a:b] * SCALE_LOG2 - row_max[:, a:b])
            stats_ref[g, 8:16, a:b] += fold(p, jnp.sum)
            p_bf = p.astype(jnp.bfloat16)
            p_buf[c, :, g * lanes + a:g * lanes + b] = p_bf
            acc[g, :, a:b] += jnp.dot(v_t, p_bf, preferred_element_type=jnp.float32)

        return step

    def over_chunks(*makers):
        @pl.loop(low, depth)
        def _(c):
            steps = [make(c) for make in makers]
            for a, b in tiles:
                for step in steps:
                    step(a, b)

    over_chunks(lambda c: score_steps(c, 0))
    for g in range(KEY_VALUE_HEADS):
        row_max = jnp.max(stats_ref[g, 0:8, :], axis=0, keepdims=True) * SCALE_LOG2
        makers = [lambda c: weight_steps(c, g, row_max)]
        if g + 1 < KEY_VALUE_HEADS:
            makers.append(lambda c: score_steps(c, g + 1))
        over_chunks(*makers)
        stats_ref[g, 0:1, :] = row_max
        stats_ref[g, 8:9, :] = jnp.sum(stats_ref[g, 8:16, :], axis=0, keepdims=True)


def near_attention(rank, q_all, near, near_core, depth):
    lanes = q_all.shape[1]
    rows = lanes // GROUP_SIZE
    packed = rows + DOC_ROWS
    chunk = PAIR * rows
    vmem = pl.BlockSpec(memory_space=pltpu.VMEM)
    smem = pl.BlockSpec(memory_space=pltpu.SMEM)
    heads = KEY_VALUE_HEADS
    return pl.pallas_call(
        near_kernel,
        out_shape=(
            jax.ShapeDtypeStruct((depth * LEVEL, packed, KV_WIDTH), jnp.bfloat16),
            jax.ShapeDtypeStruct((depth, chunk, heads * lanes), jnp.bfloat16),
            jax.ShapeDtypeStruct((heads, 16, lanes), jnp.float32),
            jax.ShapeDtypeStruct((heads, HEAD_SIZE, lanes), jnp.float32),
        ),
        in_specs=[smem] + [vmem] * 3,
        out_specs=(vmem,) * 4,
        scratch_shapes=[pltpu.VMEM((depth, chunk, lanes), jnp.float32)],
        compiler_params=pltpu.CompilerParams(vmem_limit_bytes=28 * 1024 * 1024),
        cost_estimate=pl.CostEstimate(
            flops=2 * 2 * heads * lanes * HEAD_SIZE * depth * chunk,
            bytes_accessed=4 * heads * lanes * HEAD_SIZE,
            transcendentals=heads * lanes * depth * chunk,
        ),
        name="near_attention",
    )(rank, q_all, near, near_core)


def kernel(
    rank_ref, q_all, do_all, kv_near, p_near, stats_ref, acc_near, far_0, far_1, far_2, far_3,
    att_t, dq_t, p_far, ds_buf, do_near, do_far, gb_ref, span_ref,
    kv_far, s_buf, sum_buf, factor_buf, dot_buf, acc, dq_acc,
):
    depth, chunk = p_near.shape[:2]
    rows = chunk // PAIR
    lanes = GROUP_SIZE * rows
    tiles = lane_tiles(lanes)
    rank = rank_ref[0]
    first = (rank // LEVEL - depth) * LEVEL
    spread(kv_far, 0, (far_0, far_1, far_2, far_3), rank % LEVEL)
    count = doc_count(kv_far, rows) + doc_count(kv_near, rows)
    boundary, low_block = window_start(rank, rows, first, count)
    low = jnp.maximum(low_block - first, 0) // PAIR
    span_ref[0] = low
    with_far = low == 0

    dq_acc[...] = jnp.zeros_like(dq_acc)

    @pl.when(with_far)
    def _():
        bias = mask_bias(first * rows, rank * rows, boundary, chunk, rows)

        def score(g, a, b):
            k_c = keys_of(kv_far, 0, rows, g)
            s = lax.dot_general(k_c, q_all[g, a:b, :], NT, preferred_element_type=jnp.float32)
            s = s + jnp.concatenate([bias] * ((b - a) // rows), axis=1)
            s_buf[g, :, a:b] = s
            far_max = jnp.max(fold(s, jnp.max), axis=0, keepdims=True) * SCALE_LOG2
            factor_buf[g, 0:1, a:b] = jnp.maximum(stats_ref[g, 0:1, a:b], far_max)

        def weight(g, a, b):
            v_t = keys_of(kv_far, 0, rows, KEY_VALUE_HEADS + g).T
            top = factor_buf[g, 0:1, a:b]
            factor = jnp.exp2(stats_ref[g, 0:1, a:b] - top)
            p = jnp.exp2(s_buf[g, :, a:b] * SCALE_LOG2 - top)
            p_bf = p.astype(jnp.bfloat16)
            p_far[0, :, g * lanes + a:g * lanes + b] = p_bf
            total = jnp.sum(fold(p, jnp.sum), axis=0, keepdims=True)
            sum_buf[g, 0:1, a:b] = stats_ref[g, 8:9, a:b] * factor + total
            factor_buf[g, 0:1, a:b] = factor
            acc[g, :, a:b] = acc_near[g, :, a:b] * factor + jnp.dot(
                v_t, p_bf, preferred_element_type=jnp.float32
            )

        for a, b in tiles:
            score(0, a, b)
        for g in range(KEY_VALUE_HEADS):
            for a, b in tiles:
                weight(g, a, b)
                if g + 1 < KEY_VALUE_HEADS:
                    score(g + 1, a, b)

    @pl.when(jnp.logical_not(with_far))
    def _():
        sum_buf[:, 0:1, :] = stats_ref[:, 8:9, :]
        factor_buf[:, 0:1, :] = jnp.ones((KEY_VALUE_HEADS, 1, lanes), jnp.float32)
        acc[...] = acc_near[...]

    for g in range(KEY_VALUE_HEADS):
        inverse = 1.0 / sum_buf[g, 0:1, :]
        factor = factor_buf[g, 0:1, :]
        for n in range(GROUP_SIZE):
            at = slice(n * rows, (n + 1) * rows)
            att = (acc[g, :, at] * inverse[:, at]).astype(jnp.bfloat16)
            att_t[g, :, at] = att
            do_n = do_all[g, :, at].astype(jnp.float32)
            dot_n = jnp.sum(do_n * att.astype(jnp.float32), axis=0, keepdims=True) * inverse[:, at]
            do_n = do_n * inverse[:, at]
            dot_buf[g, 0:1, at] = dot_n
            dot_buf[g, 1:2, at] = dot_n * factor[:, at]
            do_far[g, :, at] = do_n.astype(jnp.bfloat16)
            do_near[g, :, at] = (do_n * factor[:, at]).astype(jnp.bfloat16)

    def gradient_steps(g, c, kv_buf, at, p_buf, do_t, row):
        v_c = keys_of(kv_buf, at, rows, KEY_VALUE_HEADS + g)
        k_t = keys_of(kv_buf, at, rows, g).T

        def step(a, b):
            where = slice(g * lanes + a, g * lanes + b)
            d_p = jnp.dot(v_c, do_t[g, :, a:b], preferred_element_type=jnp.float32)
            p = p_buf[at, :, where].astype(jnp.float32)
            d_s = (p * (d_p - dot_buf[g, row:row + 1, a:b])).astype(jnp.bfloat16)
            ds_buf[c, :, where] = d_s
            dq_acc[g, :, a:b] += jnp.dot(k_t, d_s, preferred_element_type=jnp.float32)

        return step

    def gradients(c, kv_buf, at, p_buf, do_t, row):
        steps = [
            gradient_steps(g, c, kv_buf, at, p_buf, do_t, row) for g in range(KEY_VALUE_HEADS)
        ]
        for a, b in tiles:
            for step in steps:
                step(a, b)

    @pl.when(with_far)
    def _():
        gradients(0, kv_far, 0, p_far, do_far, 0)

    @pl.loop(jnp.maximum(low, 1), depth + 1)
    def _(c):
        gradients(c, kv_near, c - 1, p_near, do_near, 1)

    gb_ref[...] = jnp.zeros_like(gb_ref)
    ones = jnp.ones((8, rows), jnp.bfloat16)
    for g in range(KEY_VALUE_HEADS):
        for n in range(GROUP_SIZE):
            columns = slice(n * rows, (n + 1) * rows)
            d_q = (dq_acc[g, :, columns] * SCALE).astype(jnp.bfloat16)
            dq_t[g, :, columns] = d_q
            row, at = divmod(head_columns(g, n).start, KV_WIDTH)
            sums = lax.dot_general(ones, d_q, NT, preferred_element_type=jnp.float32)
            gb_ref[row:row + 1, at:at + HEAD_SIZE] = sums[0:1]


def rows_kernel(att_t, dq_t, att_ref, dq_ref):
    rows = att_ref.shape[0]
    for g in range(KEY_VALUE_HEADS):
        for n in range(GROUP_SIZE):
            at = slice(n * rows, (n + 1) * rows)
            att_ref[:, head_columns(g, n)] = att_t[g, :, at].T
            dq_ref[:, head_columns(g, n)] = dq_t[g, :, at].T


def row_results(att_t, dq_t):
    rows = att_t.shape[2] // GROUP_SIZE
    width = QUERY_HEADS * HEAD_SIZE
    vmem = pl.BlockSpec(memory_space=pltpu.VMEM)
    return pl.pallas_call(
        rows_kernel,
        out_shape=(jax.ShapeDtypeStruct((rows, width), jnp.bfloat16),) * 2,
        in_specs=[vmem] * 2,
        out_specs=(vmem,) * 2,
        compiler_params=pltpu.CompilerParams(vmem_limit_bytes=8 * 1024 * 1024),
        cost_estimate=pl.CostEstimate(
            flops=2 * rows * width, bytes_accessed=8 * rows * width, transcendentals=0
        ),
        name="row_results",
    )(att_t, dq_t)


def attention(rank, q_all, do_all, kv_near, p_near, stats, acc_near, far):
    lanes = q_all.shape[1]
    rows = lanes // GROUP_SIZE
    width = QUERY_HEADS * HEAD_SIZE
    packed = rows + DOC_ROWS
    depth, chunk = p_near.shape[:2]
    vmem = pl.BlockSpec(memory_space=pltpu.VMEM)
    smem = pl.BlockSpec(memory_space=pltpu.SMEM)
    heads = KEY_VALUE_HEADS
    return pl.pallas_call(
        kernel,
        out_shape=(
            jax.ShapeDtypeStruct((heads, HEAD_SIZE, lanes), jnp.bfloat16),
            jax.ShapeDtypeStruct((heads, HEAD_SIZE, lanes), jnp.bfloat16),
            jax.ShapeDtypeStruct((1, chunk, heads * lanes), jnp.bfloat16),
            jax.ShapeDtypeStruct((depth + 1, chunk, heads * lanes), jnp.bfloat16),
            jax.ShapeDtypeStruct((heads, HEAD_SIZE, lanes), jnp.bfloat16),
            jax.ShapeDtypeStruct((heads, HEAD_SIZE, lanes), jnp.bfloat16),
            jax.ShapeDtypeStruct((-(-width // KV_WIDTH), KV_WIDTH), jnp.float32),
            jax.ShapeDtypeStruct((1,), jnp.int32),
        ),
        in_specs=[smem] + [vmem] * (6 + len(far)),
        out_specs=(vmem,) * 7 + (smem,),
        scratch_shapes=[
            pltpu.VMEM((LEVEL, packed, KV_WIDTH), jnp.bfloat16),
            pltpu.VMEM((heads, chunk, lanes), jnp.float32),
            pltpu.VMEM((heads, 8, lanes), jnp.float32),
            pltpu.VMEM((heads, 8, lanes), jnp.float32),
            pltpu.VMEM((heads, 8, lanes), jnp.float32),
            pltpu.VMEM((heads, HEAD_SIZE, lanes), jnp.float32),
            pltpu.VMEM((heads, HEAD_SIZE, lanes), jnp.float32),
        ],
        compiler_params=pltpu.CompilerParams(vmem_limit_bytes=28 * 1024 * 1024),
        cost_estimate=pl.CostEstimate(
            flops=2 * 2 * width * HEAD_SIZE * (depth + 2) * chunk,
            bytes_accessed=8 * rows * width,
            transcendentals=0,
        ),
        name="attention",
    )(rank, q_all, do_all, kv_near, p_near, stats, acc_near, *far)


def level_kernel(
    level, p_at, rank_ref, span_ref, p_buf, ds_buf, q_all, do_t, keep_ref, send_ref
):
    chunk = p_buf.shape[1]
    rows = chunk // PAIR
    lanes = GROUP_SIZE * rows
    inner = rank_ref[0] % LEVEL
    my_core = inner % 2
    my_x = inner // 2
    active = level >= span_ref[0]

    @pl.when(active)
    def _():
        for g in range(KEY_VALUE_HEADS):
            where = slice(g * lanes, (g + 1) * lanes)
            d_key = jnp.dot(
                ds_buf[level, :, where], q_all[g], preferred_element_type=jnp.float32
            ) * SCALE
            d_value = lax.dot_general(
                p_buf[p_at, :, where], do_t[g], NT, preferred_element_type=jnp.float32
            )
            for value, column in ((d_key, g), (d_value, KEY_VALUE_HEADS + g)):
                columns = slice(column * HEAD_SIZE, (column + 1) * HEAD_SIZE)
                for x_at in range(2):
                    one = value[2 * x_at * rows:(2 * x_at + 1) * rows]
                    two = value[(2 * x_at + 1) * rows:(2 * x_at + 2) * rows]
                    place = (x_at + my_x) % 2
                    at = pl.ds(pl.multiple_of(place * rows, rows), rows)
                    keep_ref[at, columns] = jnp.where(my_core == 0, one, two)
                    send_ref[at, columns] = jnp.where(my_core == 0, two, one).astype(jnp.bfloat16)

    @pl.when(jnp.logical_not(active))
    def _():
        keep_ref[...] = jnp.zeros_like(keep_ref)
        send_ref[...] = jnp.zeros_like(send_ref)


def level_gradients(level, p_at, rank, span, p_all, ds_all, q_all, do_t):
    chunk, width = p_all.shape[1:]
    rows = chunk // PAIR
    vmem = pl.BlockSpec(memory_space=pltpu.VMEM)
    smem = pl.BlockSpec(memory_space=pltpu.SMEM)
    return pl.pallas_call(
        functools.partial(level_kernel, level, p_at),
        out_shape=(
            jax.ShapeDtypeStruct((2 * rows, KV_WIDTH), jnp.float32),
            jax.ShapeDtypeStruct((2 * rows, KV_WIDTH), jnp.bfloat16),
        ),
        in_specs=[smem, smem] + [vmem] * 4,
        out_specs=(vmem, vmem),
        compiler_params=pltpu.CompilerParams(vmem_limit_bytes=28 * 1024 * 1024),
        cost_estimate=pl.CostEstimate(
            flops=LEVEL * rows * width * HEAD_SIZE // 4,
            bytes_accessed=LEVEL * rows * width // 4,
            transcendentals=0,
        ),
        name="level_gradients",
    )(rank, span, p_all, ds_all, q_all, do_t)


def shifted(value, steps):
    count = lax.axis_size("ctx")
    first, last = max(0, -steps), min(count, count - steps)
    return lax.ppermute(value, "ctx", [(at, at + steps) for at in range(first, last)])


def rotated(value, steps):
    count = lax.axis_size("ctx")
    return lax.ppermute(value, "ctx", [(at, (at + steps) % count) for at in range(count)])


def swapped(value, bit, axis="ctx"):
    return lax.ppermute(value, axis, [(at, at ^ bit) for at in range(lax.axis_size(axis))])


def bias_rows(rows):
    high = lax.reduce_precision(rows, 8, 7)
    both = jnp.concatenate([high, rows - high]).astype(jnp.bfloat16)
    return jnp.pad(both, ((0, -both.shape[0] % 16), (0, 0)))


def local(query_in, key_in, value_input, output_gradient, doc_ids, query_bias):
    rows = query_in.shape[1]
    shards = lax.axis_size("ctx")
    depth = window_levels(shards)
    rank = lax.axis_index("ctx").astype(jnp.int32)
    own = pack(key_in[0], value_input[0], doc_ids)

    ups = [shifted(own, LEVEL * step) for step in range(1, depth + 1)]
    x_own = swapped(own, 2)
    q_all, do_all, own = prepare(query_in[0], query_bias[None], output_gradient[0], own)
    ups[0], x_own, q_all, do_all = lax.optimization_barrier((ups[0], x_own, q_all, do_all))
    near = [own, x_own]
    for up in ups[:-1]:
        near += [up, swapped(up, 2)]
    x_far = swapped(ups[-1], 2)
    far_up, near = lax.optimization_barrier((ups[-1], near))
    near = jnp.concatenate(near, axis=0)
    near_core = swapped(near, 1)
    core_far = swapped(far_up, 1)
    rank = rank.reshape(1)
    kv_near, p_near, stats, acc_near = near_attention(rank, q_all, near, near_core, depth)
    x_far, p_near = lax.optimization_barrier((x_far, p_near))
    far = [far_up, x_far, core_far, swapped(x_far, 1)]
    att_t, dq_t, p_far, ds_all, do_near, do_far, bias_part, span = attention(
        rank, q_all, do_all, kv_near, p_near, stats, acc_near, far
    )

    levels = shards // LEVEL
    carried = levels == 4 and depth == 2
    bit = 1
    while bit < lax.axis_size("dp"):
        bias_part = bias_part + swapped(bias_part, bit, "dp")
        bit *= 2
    bias_total = bias_part

    def joined(value):
        return jnp.concatenate([value, bias_rows(bias_total)], axis=0) if carried else value

    def bias_of(got):
        return got[rows:rows + half_rows].astype(jnp.float32) + got[
            rows + half_rows:rows + 2 * half_rows
        ].astype(jnp.float32)

    half_rows = bias_part.shape[0]
    sends = [None] * (depth + 1)
    keeps = [None] * (depth + 1)
    for step in range(depth, -1, -1):
        if step == depth:
            keep, send = level_gradients(0, 0, rank, span, p_far, ds_all, q_all, do_far)
        else:
            level = depth - step
            keep, send = level_gradients(
                level, level - 1, rank, span, p_near, ds_all, q_all, do_near
            )
        send, ds_all = lax.optimization_barrier((send, ds_all))
        if step == max(depth - 1, 0) and carried:
            got = swapped(jnp.concatenate([send, bias_rows(bias_total)], axis=0), 1)
            bias_total = bias_total + bias_of(got[rows:])
            got = got[:2 * rows]
        else:
            got = swapped(send, 1)
        keeps[step] = keep + got.astype(jnp.float32)
        sends[step] = send

    across = [None] * (depth + 1)
    for step in range(depth, -1, -1):
        away = keeps[step][rows:].astype(jnp.bfloat16)
        if step == depth:
            away, att_t = lax.optimization_barrier((away, att_t))
            away = joined(away)
        across[step] = swapped(away, 2)
    attended, grad_query = row_results(att_t, dq_t)
    down = [None] * (depth + 1)
    total = None
    for step in range(depth, -1, -1):
        if step == depth and carried:
            bias_total = bias_total + bias_of(across[step])
        total = keeps[step][:rows] + across[step][:rows].astype(jnp.float32)
        if step:
            sent = joined(total.astype(jnp.bfloat16))
            down[step] = (rotated if carried else shifted)(sent, -LEVEL * step)
            across[step - 1], _ = lax.optimization_barrier((across[step - 1], sent))
    if carried:
        bias_total = (
            bias_total + rotated(bias_total, LEVEL) + bias_of(down[1]) + bias_of(down[2])
        )
    else:
        bit = 1
        while bit < shards:
            bias_total = bias_total + swapped(bias_total, bit)
            bit *= 2
    bias_total = bias_total.reshape(-1)[:query_bias.shape[0]]
    down = [None if part is None else part[:rows] for part in down]
    for step in range(depth, 0, -1):
        total = total + down[step].astype(jnp.float32)
    total = total.astype(jnp.bfloat16)
    half = KEY_VALUE_HEADS * HEAD_SIZE
    return (
        attended[None],
        grad_query[None],
        total[:, :half][None],
        total[:, half:][None],
        bias_total,
    )


def solution(mesh):
    placed = (
        P("dp", "ctx", None),
        P("dp", "ctx", None),
        P("dp", "ctx", None),
        P("dp", "ctx", None),
        P("dp", "ctx"),
        P(),
    )
    return jax.shard_map(
        local,
        mesh=mesh,
        in_specs=placed,
        out_specs=(
            P("dp", "ctx", None),
            P("dp", "ctx", None),
            P("dp", "ctx", None),
            P("dp", "ctx", None),
            P(),
        ),
        check_vma=False,
    )
```

profile of v0, /device:TPU:0, one launch (start us, length us, event | category | flops | bytes accessed | tf_op | source)
XLA Modules:
  0.0 63.0 jit_solution(2039517429310096070)
XLA Ops:
  0.6 1.6 %pack.1.own_hbm = bf16[144,512]{1,0:T(8,128)(2,1)} custom-call(bf16[128,256]{1,0:T(8,128)(2,1)} %bitcast.17, bf16[128,256]{1,0:T(8,128)(2,1)} %bitcast.18, s32[1,128]{1,0:T(1,128)} %docs_hbm.1), custom_call_target="tpu_custom_call" | custom-call | tf_op jit(solution)/shard_map/pack/pallas_call | solution.py:59
  2.2 3.0 %collective-permute-start.1 = (bf16[144,512]{1,0:T(8,128)(2,1)}, bf16[144,512]{1,0:T(8,128)(2,1)S(1)}, u32[]{:S(2)}, u32[]{:S(2)}) collective-permute-start(bf16[144,512]{1,0:T(8,128)(2,1)} %pack.1.own_hbm), channel_id=1, source_target_pairs={{0,2},{1,3},{2,0},{3,1},{4,6},{5,7},{6,4},{7,5},{8,10},{9,11},{10,... | collective-permute-start | bytes 442376 | tf_op jit(solution)/shard_map/ppermute | solution.py:517
  5.2 3.5 %collective-permute-start = (bf16[144,512]{1,0:T(8,128)(2,1)}, bf16[144,512]{1,0:T(8,128)(2,1)S(1)}, u32[]{:S(2)}, u32[]{:S(2)}) collective-permute-start(bf16[144,512]{1,0:T(8,128)(2,1)} %pack.1.own_hbm), channel_id=1, source_target_pairs={{0,4},{1,5},{2,6},{3,7},{4,8},{5,9},{6,10},{7,11},{8,12},{9,13},{1... | collective-permute-start | bytes 442376 | tf_op jit(solution)/shard_map/ppermute | solution.py:508
  8.7 4.5 %collective-permute-start.2 = (bf16[144,512]{1,0:T(8,128)(2,1)}, bf16[144,512]{1,0:T(8,128)(2,1)S(1)}, u32[]{:S(2)}, u32[]{:S(2)}) collective-permute-start(bf16[144,512]{1,0:T(8,128)(2,1)} %pack.1.own_hbm), channel_id=1, source_target_pairs={{0,8},{1,9},{2,10},{3,11},{4,12},{5,13},{6,14},{7,15},{16,24},{17,... | collective-permute-start | bytes 442376 | tf_op jit(solution)/shard_map/ppermute | solution.py:508
  13.2 0.7 %broadcast_in_dim.15.bias_ref = f32[1,1792]{1,0:T(1,128)S(1)} reshape(f32[1792]{0:T(1024)} %param.11) | data formatting | bytes 14336 | tf_op jit(solution)/shard_map/broadcast_in_dim | solution.py:535
  13.9 0.0 copy-start
  13.9 0.9 %copy-done = bf16[144,512]{1,0:T(8,128)(2,1)S(1)} copy-done((bf16[144,512]{1,0:T(8,128)(2,1)S(1)}, bf16[144,512]{1,0:T(8,128)(2,1)}, u32[]{:S(2)}) %copy-start) | copy-done | bytes 147480
  14.8 0.0 copy-start.1
  14.8 1.0 %copy-done.1 = bf16[1,128,1792]{2,1,0:T(8,128)(2,1)S(1)} copy-done((bf16[1,128,1792]{2,1,0:T(8,128)(2,1)S(1)}, bf16[1,128,1792]{2,1,0:T(8,128)(2,1)}, u32[]{:S(2)}) %copy-start.1) | copy-done | bytes 458776
  15.8 0.0 copy-start.2
  15.8 1.0 %copy-done.2 = bf16[1,128,1792]{2,1,0:T(8,128)(2,1)S(1)} copy-done((bf16[1,128,1792]{2,1,0:T(8,128)(2,1)S(1)}, bf16[1,128,1792]{2,1,0:T(8,128)(2,1)}, u32[]{:S(2)}) %copy-start.2) | copy-done | bytes 458776
  16.9 1.0 %prepare.1 = (bf16[2,896,128]{2,1,0:T(8,128)(2,1)S(1)}, bf16[2,128,896]{2,1,0:T(8,128)(2,1)S(1)}, bf16[144,512]{1,0:T(8,128)(2,1)S(1)}) custom-call(bf16[128,1792]{1,0:T(8,128)(2,1)S(1)} %bitcast.15, f32[1,1792]{1,0:T(1,128)S(1)} %broadcast_in_dim.15.bias_ref, bf16[128,1792]{1,0:T(8,128)(2,1)S(1)} %bitcast.16, bf16[144,512]{1,0:T(8,128)(2,1)S(1)} %copy-done), custom_call_target="tpu_custom_call" | custom-call | flops 917504 | bytes 1835008 | tf_op jit(solution)/shard_map/prepare/pallas_call | solution.py:102
  17.9 0.0 collective-permute-done.1
  17.9 0.0 collective-permute-done
  17.9 0.6 collective-permute-start.3
  18.5 0.0 collective-permute-done.2.far_0
  18.5 4.6 %collective-permute-done.3 = bf16[144,512]{1,0:T(8,128)(2,1)S(1)} collective-permute-done((bf16[144,512]{1,0:T(8,128)(2,1)S(1)}, bf16[144,512]{1,0:T(8,128)(2,1)S(1)}, u32[]{:S(2)}, u32[]{:S(2)}) %collective-permute-start.3) | collective-permute-done | bytes 147488 | tf_op jit(solution)/shard_map/ppermute | solution.py:517
  23.2 0.1 collective-permute-start.4
  23.3 0.6 collective-permute-start.5
  23.9 0.2 collective-permute-start.6
  24.0 1.2 %collective-permute-done.4.near_core_ref = bf16[576,512]{1,0:T(8,128)(2,1)S(1)} collective-permute-done((bf16[576,512]{1,0:T(8,128)(2,1)S(1)}, bf16[576,512]{1,0:T(8,128)(2,1)S(1)}, u32[]{:S(2)}, u32[]{:S(2)}) %collective-permute-start.4) | collective-permute-done | bytes 589856 | tf_op jit(solution)/shard_map/ppermute | solution.py:517
  25.2 2.3 %near_attention.1 = (bf16[8,144,512]{2,1,0:T(8,128)(2,1)S(1)}, bf16[2,512,1792]{2,1,0:T(8,128)(2,1)S(1)}, f32[2,16,896]{2,1,0:T(8,128)S(1)}, f32[2,128,896]{2,1,0:T(8,128)S(1)}) custom-call(s32[1]{0:T(128)} %bitcast.rank_ref, bf16[2,896,128]{2,1,0:T(8,128)(2,1)S(1)} %get-tuple-element.50.q_all, ...), custom_call_target="tpu_custom_call" | custom-call | flops 939524096 | bytes 917504 | tf_op jit(solution)/shard_map/near_attention/pallas_call | solution.py:239
  27.5 2.0 %collective-permute-done.5.far_1 = bf16[144,512]{1,0:T(8,128)(2,1)S(1)} collective-permute-done((bf16[144,512]{1,0:T(8,128)(2,1)S(1)}, bf16[144,512]{1,0:T(8,128)(2,1)S(1)}, u32[]{:S(2)}, u32[]{:S(2)}) %collective-permute-start.5) | collective-permute-done | bytes 147488 | tf_op jit(solution)/shard_map/ppermute | solution.py:517
  29.5 0.0 collective-permute-start.7
  29.5 0.0 collective-permute-done.6.far_2
  29.5 1.4 %collective-permute-done.7.far_3 = bf16[144,512]{1,0:T(8,128)(2,1)S(1)} collective-permute-done((bf16[144,512]{1,0:T(8,128)(2,1)S(1)}, bf16[144,512]{1,0:T(8,128)(2,1)S(1)}, u32[]{:S(2)}, u32[]{:S(2)}) %collective-permute-start.7) | collective-permute-done | bytes 147488 | tf_op jit(solution)/shard_map/ppermute | solution.py:517
  30.9 3.4 %attention.1 = (bf16[2,128,896]{2,1,0:T(8,128)(2,1)S(1)}, bf16[2,128,896]{2,1,0:T(8,128)(2,1)S(1)}, bf16[1,512,1792]{2,1,0:T(8,128)(2,1)S(1)}, bf16[3,512,1792]{...) custom-call(s32[1]{0:T(128)} %bitcast.rank_ref, ...), custom_call_target="tpu_custom_call" | custom-call | flops 1879048192 | bytes 1835008 | tf_op jit(solution)/shard_map/attention/pallas_call | solution.py:412
  34.3 1.6 %collective-permute-start.11 = (f32[4,512]{1,0:T(4,128)S(1)}, f32[4,512]{1,0:T(4,128)S(1)}, u32[]{:S(2)}, u32[]{:S(2)}) collective-permute-start(f32[4,512]{1,0:T(4,128)S(1)} %get-tuple-element.87), channel_id=1, source_target_pairs={{0,16},{16,0},{1,17},{17,1},{2,18},{18,2},{3,19},{19,3},{4,20},{20... | collective-permute-start | bytes 24584 | tf_op jit(solution)/shard_map/ppermute | solution.py:517
  35.8 0.7 %level_gradients.3 = (f32[256,512]{1,0:T(8,128)S(1)}, bf16[256,512]{1,0:T(8,128)(2,1)S(1)}) custom-call(s32[1]{0:T(128)} %bitcast.rank_ref, s32[1]{0:T(128)} %get-tuple-element.66.span_ref, bf16[1,512,1792]{2,1,0:T(8,128)(2,1)S(1)} %get-tuple-element.67.p_buf, bf16[3,512,1792]{2,1,0:T(8,128)(2,1)S(1)} %get-tuple-element.81.ds_buf, ...), custom_call_target="tpu_custom_call" | custom-call | flops 29360128 | bytes 229376 | tf_op jit(solution)/shard_map/level_gradients/pallas_call | solution.py:487
  36.6 0.1 collective-permute-start.8
  36.6 0.7 %level_gradients.4 = (f32[256,512]{1,0:T(8,128)S(1)}, bf16[256,512]{1,0:T(8,128)(2,1)S(1)}) custom-call(s32[1]{0:T(128)} %bitcast.rank_ref, s32[1]{0:T(128)} %get-tuple-element.66.span_ref, bf16[2,512,1792]{2,1,0:T(8,128)(2,1)S(1)} %get-tuple-element.61.p_near.p_buf, bf16[3,512,1792]{2,1,0:T(8,128)(2,1)S(1)} %get-tuple-element.81.ds_buf, ...), custom_call_target="tpu_custom_call" | custom-call | flops 29360128 | bytes 229376 | tf_op jit(solution)/shard_map/level_gradients/pallas_call | solution.py:487
  37.4 0.6 collective-permute-done.11
  38.0 0.1 collective-permute-start.12
  38.1 1.8 %level_gradients.5 = (f32[256,512]{1,0:T(8,128)S(1)}, bf16[256,512]{1,0:T(8,128)(2,1)S(1)}) custom-call(s32[1]{0:T(128)} %bitcast.rank_ref, s32[1]{0:T(128)} %get-tuple-element.66.span_ref, bf16[2,512,1792]{2,1,0:T(8,128)(2,1)S(1)} %get-tuple-element.61.p_near.p_buf, bf16[3,512,1792]{2,1,0:T(8,128)(2,1)S(1)} %get-tuple-element.81.ds_buf, ...), custom_call_target="tpu_custom_call" | custom-call | flops 29360128 | bytes 229376 | tf_op jit(solution)/shard_map/level_gradients/pallas_call | solution.py:487
  39.9 0.6 collective-permute-start.9
  40.5 0.0 collective-permute-done.8
  40.5 0.1 convert_add_fusion.2
  40.6 0.0 collective-permute-done.12
  40.6 0.6 collective-permute-start.14
  41.2 0.1 convert_add_fusion
  41.3 1.6 %collective-permute-start.13 = (bf16[128,512]{1,0:T(8,128)(2,1)S(1)}, bf16[128,512]{1,0:T(8,128)(2,1)S(1)}, u32[]{:S(2)}, u32[]{:S(2)}) collective-permute-start(bf16[128,512]{1,0:T(8,128)(2,1)S(1)} %slice.153), channel_id=1, source_target_pairs={{0,2},{1,3},{2,0},{3,1},{4,6},{5,7},{6,4},{7,5},{8,10},{9,11},{10,... | collective-permute-start | bytes 393224 | tf_op jit(solution)/shard_map/ppermute | solution.py:517
  42.9 4.5 %collective-permute-done.14 = bf16[144,512]{1,0:T(8,128)(2,1)S(1)} collective-permute-done((bf16[144,512]{1,0:T(8,128)(2,1)S(1)}, bf16[144,512]{1,0:T(8,128)(2,1)S(1)}, u32[]{:S(2)}, u32[]{:S(2)}) %collective-permute-start.14) | collective-permute-done | bytes 147488 | tf_op jit(solution)/shard_map/ppermute | solution.py:517
  47.5 6.0 %collective-permute-start.15 = (bf16[144,512]{1,0:T(8,128)(2,1)S(1)}, bf16[144,512]{1,0:T(8,128)(2,1)S(1)}, u32[]{:S(2)}, u32[]{:S(2)}) collective-permute-start(bf16[144,512]{1,0:T(8,128)(2,1)S(1)} %pad_maximum_fusion.2), channel_id=1, source_target_pairs={{0,8},{1,9},{2,10},{3,11},{4,12},{5,13},{6,14},{7,15},{8,0},{9,1},... | collective-permute-start | bytes 442376 | tf_op jit(solution)/shard_map/ppermute | solution.py:513
  53.5 0.0 collective-permute-done.13
  53.5 1.8 %collective-permute-start.16 = (bf16[144,512]{1,0:T(8,128)(2,1)S(1)}, bf16[144,512]{1,0:T(8,128)(2,1)S(1)}, u32[]{:S(2)}, u32[]{:S(2)}) collective-permute-start(bf16[144,512]{1,0:T(8,128)(2,1)S(1)} %pad_maximum_fusion.1), channel_id=1, source_target_pairs={{0,12},{1,13},{2,14},{3,15},{4,0},{5,1},{6,2},{7,3},{8,4},{9,5},{1... | collective-permute-start | bytes 442376 | tf_op jit(solution)/shard_map/ppermute | solution.py:513
  55.3 0.0 collective-permute-done.9
  55.4 0.1 convert_add_fusion.1
  55.5 0.6 collective-permute-start.10
  56.1 0.0 collective-permute-start.17
  56.1 1.2 %row_results.1 = (bf16[128,1792]{1,0:T(8,128)(2,1)}, bf16[128,1792]{1,0:T(8,128)(2,1)}) custom-call(bf16[2,128,896]{2,1,0:T(8,128)(2,1)S(1)} %get-tuple-element.74.att_t, bf16[2,128,896]{2,1,0:T(8,128)(2,1)S(1)} %get-tuple-element.75.dq_t), custom_call_target="tpu_custom_call" | custom-call | flops 458752 | bytes 1835008 | tf_op jit(solution)/shard_map/row_results/pallas_call | solution.py:390
  57.3 3.2 %collective-permute-done.10 = bf16[128,512]{1,0:T(8,128)(2,1)S(1)} collective-permute-done((bf16[128,512]{1,0:T(8,128)(2,1)S(1)}, bf16[128,512]{1,0:T(8,128)(2,1)S(1)}, u32[]{:S(2)}, u32[]{:S(2)}) %collective-permute-start.10) | collective-permute-done | bytes 131104 | tf_op jit(solution)/shard_map/ppermute | solution.py:517
  60.5 1.1 %collective-permute-done.17 = f32[4,512]{1,0:T(4,128)S(1)} collective-permute-done((f32[4,512]{1,0:T(4,128)S(1)}, f32[4,512]{1,0:T(4,128)S(1)}, u32[]{:S(2)}, u32[]{:S(2)}) %collective-permute-start.17) | collective-permute-done | bytes 8224 | tf_op jit(solution)/shard_map/ppermute | solution.py:513
  61.6 0.0 collective-permute-done.16
  61.6 0.0 collective-permute-done.15
  61.6 0.6 copy.11
  62.2 0.1 fusion.4
  62.3 0.7 %slice_bitcast_fusion = (bf16[1,128,256]{2,1,0:T(8,128)(2,1)}, bf16[1,128,256]{2,1,0:T(8,128)(2,1)}) fusion(bf16[128,512]{1,0:T(8,128)(2,1)S(1)} %fusion.4), kind=kLoop, calls=%fused_computation.18 | loop fusion | bytes 262144 | tf_op jit(solution)/shard_map/broadcast_in_dim | solution.py:627
  (22 shorter events, 0.3 us)
Async XLA Ops:
  2.2 15.7 %collective-permute-start.1 = (bf16[144,512]{1,0:T(8,128)(2,1)}, bf16[144,512]{1,0:T(8,128)(2,1)S(1)}, u32[]{:S(2)}, u32[]{:S(2)}) collective-permute-start(bf16[144,512]{1,0:T(8,128)(2,1)} %pack.1.own_hbm), channel_id=1, source_target_pairs={{0,2},{1,3},{2,0},{3,1},{4,6},{5,7},{6,4},{7,5},{8,10},{9,11},{10,... | collective-permute-start | bytes 442376 | tf_op jit(solution)/shard_map/ppermute | solution.py:517
  5.2 12.7 %collective-permute-start = (bf16[144,512]{1,0:T(8,128)(2,1)}, bf16[144,512]{1,0:T(8,128)(2,1)S(1)}, u32[]{:S(2)}, u32[]{:S(2)}) collective-permute-start(bf16[144,512]{1,0:T(8,128)(2,1)} %pack.1.own_hbm), channel_id=1, source_target_pairs={{0,4},{1,5},{2,6},{3,7},{4,8},{5,9},{6,10},{7,11},{8,12},{9,13},{1... | collective-permute-start | bytes 442376 | tf_op jit(solution)/shard_map/ppermute | solution.py:508
  8.7 9.8 %collective-permute-start.2 = (bf16[144,512]{1,0:T(8,128)(2,1)}, bf16[144,512]{1,0:T(8,128)(2,1)S(1)}, u32[]{:S(2)}, u32[]{:S(2)}) collective-permute-start(bf16[144,512]{1,0:T(8,128)(2,1)} %pack.1.own_hbm), channel_id=1, source_target_pairs={{0,8},{1,9},{2,10},{3,11},{4,12},{5,13},{6,14},{7,15},{16,24},{17,... | collective-permute-start | bytes 442376 | tf_op jit(solution)/shard_map/ppermute | solution.py:508
  13.9 0.9 %copy-start = (bf16[144,512]{1,0:T(8,128)(2,1)S(1)}, bf16[144,512]{1,0:T(8,128)(2,1)}, u32[]{:S(2)}) copy-start(bf16[144,512]{1,0:T(8,128)(2,1)} %pack.1.own_hbm) | copy-start | bytes 442372
  14.8 1.0 %copy-start.1 = (bf16[1,128,1792]{2,1,0:T(8,128)(2,1)S(1)}, bf16[1,128,1792]{2,1,0:T(8,128)(2,1)}, u32[]{:S(2)}) copy-start(bf16[1,128,1792]{2,1,0:T(8,128)(2,1)} %param.6) | copy-start | bytes 1376260
  15.8 1.0 %copy-start.2 = (bf16[1,128,1792]{2,1,0:T(8,128)(2,1)S(1)}, bf16[1,128,1792]{2,1,0:T(8,128)(2,1)}, u32[]{:S(2)}) copy-start(bf16[1,128,1792]{2,1,0:T(8,128)(2,1)} %param.9) | copy-start | bytes 1376260
  17.9 5.2 %collective-permute-start.3 = (bf16[144,512]{1,0:T(8,128)(2,1)S(1)}, bf16[144,512]{1,0:T(8,128)(2,1)S(1)}, u32[]{:S(2)}, u32[]{:S(2)}) collective-permute-start(bf16[144,512]{1,0:T(8,128)(2,1)S(1)} %collective-permute-done), channel_id=1, source_target_pairs={{0,2},{1,3},{2,0},{3,1},{4,6},{5,7},{6,4},{7,5},{8,10},{9,11},{10,... | collective-permute-start | bytes 442376 | tf_op jit(solution)/shard_map/ppermute | solution.py:517
  23.2 2.1 %collective-permute-start.4 = (bf16[576,512]{1,0:T(8,128)(2,1)S(1)}, bf16[576,512]{1,0:T(8,128)(2,1)S(1)}, u32[]{:S(2)}, u32[]{:S(2)}) collective-permute-start(bf16[576,512]{1,0:T(8,128)(2,1)S(1)} %constant_dynamic-update-slice_fusion.near_ref), channel_id=1, source_target_pairs={{0,1},{1,0},{2,3},{3,2},{4,5},{5,4},{6,7},{7,6},{8,9},{9,8},{10,11... | collective-permute-start | bytes 1769480 | tf_op jit(solution)/shard_map/ppermute | solution.py:517
  23.3 6.3 %collective-permute-start.5 = (bf16[144,512]{1,0:T(8,128)(2,1)S(1)}, bf16[144,512]{1,0:T(8,128)(2,1)S(1)}, u32[]{:S(2)}, u32[]{:S(2)}) collective-permute-start(bf16[144,512]{1,0:T(8,128)(2,1)S(1)} %collective-permute-done.2.far_0), channel_id=1, source_target_pairs={{0,2},{1,3},{2,0},{3,1},{4,6},{5,7},{6,4},{7,5},{8,10},{9,11},{10,... | collective-permute-start | bytes 442376 | tf_op jit(solution)/shard_map/ppermute | solution.py:517
  23.9 5.7 %collective-permute-start.6 = (bf16[144,512]{1,0:T(8,128)(2,1)S(1)}, bf16[144,512]{1,0:T(8,128)(2,1)S(1)}, u32[]{:S(2)}, u32[]{:S(2)}) collective-permute-start(bf16[144,512]{1,0:T(8,128)(2,1)S(1)} %collective-permute-done.2.far_0), channel_id=1, source_target_pairs={{0,1},{1,0},{2,3},{3,2},{4,5},{5,4},{6,7},{7,6},{8,9},{9,8},{10,11... | collective-permute-start | bytes 442376 | tf_op jit(solution)/shard_map/ppermute | solution.py:517
  29.5 1.4 %collective-permute-start.7 = (bf16[144,512]{1,0:T(8,128)(2,1)S(1)}, bf16[144,512]{1,0:T(8,128)(2,1)S(1)}, u32[]{:S(2)}, u32[]{:S(2)}) collective-permute-start(bf16[144,512]{1,0:T(8,128)(2,1)S(1)} %collective-permute-done.5.far_1), channel_id=1, source_target_pairs={{0,1},{1,0},{2,3},{3,2},{4,5},{5,4},{6,7},{7,6},{8,9},{9,8},{10,11... | collective-permute-start | bytes 442376 | tf_op jit(solution)/shard_map/ppermute | solution.py:517
  34.3 3.7 %collective-permute-start.11 = (f32[4,512]{1,0:T(4,128)S(1)}, f32[4,512]{1,0:T(4,128)S(1)}, u32[]{:S(2)}, u32[]{:S(2)}) collective-permute-start(f32[4,512]{1,0:T(4,128)S(1)} %get-tuple-element.87), channel_id=1, source_target_pairs={{0,16},{16,0},{1,17},{17,1},{2,18},{18,2},{3,19},{19,3},{4,20},{20... | collective-permute-start | bytes 24584 | tf_op jit(solution)/shard_map/ppermute | solution.py:517
  36.6 3.9 %collective-permute-start.8 = (bf16[256,512]{1,0:T(8,128)(2,1)S(1)}, bf16[256,512]{1,0:T(8,128)(2,1)S(1)}, u32[]{:S(2)}, u32[]{:S(2)}) collective-permute-start(bf16[256,512]{1,0:T(8,128)(2,1)S(1)} %get-tuple-element.72), channel_id=1, source_target_pairs={{0,1},{1,0},{2,3},{3,2},{4,5},{5,4},{6,7},{7,6},{8,9},{9,8},{10,11... | collective-permute-start | bytes 786440 | tf_op jit(solution)/shard_map/ppermute | solution.py:517
  38.0 2.5 %collective-permute-start.12 = (bf16[272,512]{1,0:T(8,128)(2,1)S(1)}, bf16[272,512]{1,0:T(8,128)(2,1)S(1)}, u32[]{:S(2)}, u32[]{:S(2)}) collective-permute-start(bf16[272,512]{1,0:T(8,128)(2,1)S(1)} %pad_maximum_fusion), channel_id=1, source_target_pairs={{0,1},{1,0},{2,3},{3,2},{4,5},{5,4},{6,7},{7,6},{8,9},{9,8},{10,11... | collective-permute-start | bytes 835592 | tf_op jit(solution)/shard_map/ppermute | solution.py:517
  39.9 15.5 %collective-permute-start.9 = (bf16[256,512]{1,0:T(8,128)(2,1)S(1)}, bf16[256,512]{1,0:T(8,128)(2,1)S(1)}, u32[]{:S(2)}, u32[]{:S(2)}) collective-permute-start(bf16[256,512]{1,0:T(8,128)(2,1)S(1)} %get-tuple-element.84), channel_id=1, source_target_pairs={{0,1},{1,0},{2,3},{3,2},{4,5},{5,4},{6,7},{7,6},{8,9},{9,8},{10,11... | collective-permute-start | bytes 786440 | tf_op jit(solution)/shard_map/ppermute | solution.py:517
  40.6 6.8 %collective-permute-start.14 = (bf16[144,512]{1,0:T(8,128)(2,1)S(1)}, bf16[144,512]{1,0:T(8,128)(2,1)S(1)}, u32[]{:S(2)}, u32[]{:S(2)}) collective-permute-start(bf16[144,512]{1,0:T(8,128)(2,1)S(1)} %pad_maximum_fusion.3), channel_id=1, source_target_pairs={{0,2},{1,3},{2,0},{3,1},{4,6},{5,7},{6,4},{7,5},{8,10},{9,11},{10,... | collective-permute-start | bytes 442376 | tf_op jit(solution)/shard_map/ppermute | solution.py:517
  41.3 12.2 %collective-permute-start.13 = (bf16[128,512]{1,0:T(8,128)(2,1)S(1)}, bf16[128,512]{1,0:T(8,128)(2,1)S(1)}, u32[]{:S(2)}, u32[]{:S(2)}) collective-permute-start(bf16[128,512]{1,0:T(8,128)(2,1)S(1)} %slice.153), channel_id=1, source_target_pairs={{0,2},{1,3},{2,0},{3,1},{4,6},{5,7},{6,4},{7,5},{8,10},{9,11},{10,... | collective-permute-start | bytes 393224 | tf_op jit(solution)/shard_map/ppermute | solution.py:517
  47.5 14.1 %collective-permute-start.15 = (bf16[144,512]{1,0:T(8,128)(2,1)S(1)}, bf16[144,512]{1,0:T(8,128)(2,1)S(1)}, u32[]{:S(2)}, u32[]{:S(2)}) collective-permute-start(bf16[144,512]{1,0:T(8,128)(2,1)S(1)} %pad_maximum_fusion.2), channel_id=1, source_target_pairs={{0,8},{1,9},{2,10},{3,11},{4,12},{5,13},{6,14},{7,15},{8,0},{9,1},... | collective-permute-start | bytes 442376 | tf_op jit(solution)/shard_map/ppermute | solution.py:513
  53.5 8.1 %collective-permute-start.16 = (bf16[144,512]{1,0:T(8,128)(2,1)S(1)}, bf16[144,512]{1,0:T(8,128)(2,1)S(1)}, u32[]{:S(2)}, u32[]{:S(2)}) collective-permute-start(bf16[144,512]{1,0:T(8,128)(2,1)S(1)} %pad_maximum_fusion.1), channel_id=1, source_target_pairs={{0,12},{1,13},{2,14},{3,15},{4,0},{5,1},{6,2},{7,3},{8,4},{9,5},{1... | collective-permute-start | bytes 442376 | tf_op jit(solution)/shard_map/ppermute | solution.py:513
  55.5 5.0 %collective-permute-start.10 = (bf16[128,512]{1,0:T(8,128)(2,1)S(1)}, bf16[128,512]{1,0:T(8,128)(2,1)S(1)}, u32[]{:S(2)}, u32[]{:S(2)}) collective-permute-start(bf16[128,512]{1,0:T(8,128)(2,1)S(1)} %slice.154), channel_id=1, source_target_pairs={{0,2},{1,3},{2,0},{3,1},{4,6},{5,7},{6,4},{7,5},{8,10},{9,11},{10,... | collective-permute-start | bytes 393224 | tf_op jit(solution)/shard_map/ppermute | solution.py:517
  56.1 5.6 %collective-permute-start.17 = (f32[4,512]{1,0:T(4,128)S(1)}, f32[4,512]{1,0:T(4,128)S(1)}, u32[]{:S(2)}, u32[]{:S(2)}) collective-permute-start(f32[4,512]{1,0:T(4,128)S(1)} %get-tuple-element.92), channel_id=1, source_target_pairs={{0,4},{1,5},{2,6},{3,7},{4,8},{5,9},{6,10},{7,11},{8,12},{9,13},{1... | collective-permute-start | bytes 24584 | tf_op jit(solution)/shard_map/ppermute | solution.py:513
where the time goes:
time: 64.1 us; the launch traced here: 63 us
  starting transfers between devices  25.2 us (39%)
  waiting for transfers between devices  18.7 us (29%)
  Pallas kernels  12.6 us (20%)
  local copies, waits for them, and re-layouts  5.02 us (8%)
  between operations  0.93 us (1%)
    ppermute x13, waiting for transfers between devices, swapped(): lax.ppermute(value, axis, [(at, at ^ bit) for at in range(lax.axis_size(a...  17.6 us
    ppermute x13, starting transfers between devices, swapped(): lax.ppermute(value, axis, [(at, at ^ bit) for at in range(lax.axis_size(a...  9.48 us
    ppermute x2, starting transfers between devices, shifted(): lax.ppermute(value, 'ctx', [(at, at + steps) for at in range(first, last)])  7.97 us
    ppermute x3, starting transfers between devices, rotated(): lax.ppermute(value, 'ctx', [(at, (at + steps) % count) for at in range(co...  7.79 us
    unnamed x10, local copies, waits for them, and re-layouts  3.58 us
    pallas_call x1, Pallas kernels, attention(): pl.pallas_call(kernel, out_shape=(jax.ShapeDtypeStruct((heads, HEAD_SIZE,...  3.36 us
    pallas_call x3, Pallas kernels, level_gradients(): pl.pallas_call(functools.partial(level_kernel, level, p_at), out_shape=(j...  3.2 us
    pallas_call x1, Pallas kernels, near_attention(): pl.pallas_call(near_kernel, out_shape=(jax.ShapeDtypeStruct((depth * LEVE...  2.26 us
  transfers between devices with their start and end apart: 18, of which 8 were waited for; matrix products, arithmetic and copies ran while one was open for 2% of the time, Pallas kernels for 12%

commit v1 on v0

--- a/solution.py
+++ b/solution.py
@@ -339,8 +339,7 @@
         def step(a, b):
             where = slice(g * lanes + a, g * lanes + b)
             d_p = jnp.dot(v_c, do_t[g, :, a:b], preferred_element_type=jnp.float32)
-            p = p_buf[at, :, where].astype(jnp.float32)
-            d_s = (p * (d_p - dot_buf[g, row:row + 1, a:b])).astype(jnp.bfloat16)
+            d_s = p_buf[at, :, where] * (d_p - dot_buf[g, row:row + 1, a:b]).astype(jnp.bfloat16)
             ds_buf[c, :, where] = d_s
             dq_acc[g, :, a:b] += jnp.dot(k_t, d_s, preferred_element_type=jnp.float32)
 

time: 64.1 us -> 63.5 us (level)
  no operation moved by 1% of the time
where the time goes in v1:
time: 63.5 us; the launch traced here: 63 us
  starting transfers between devices  25.2 us (40%)
  waiting for transfers between devices  18.7 us (29%)
  Pallas kernels  12.6 us (20%)
  local copies, waits for them, and re-layouts  5.02 us (8%)
  between operations  0.93 us (1%)
    ppermute x13, waiting for transfers between devices, swapped(): lax.ppermute(value, axis, [(at, at ^ bit) for at in range(lax.axis_size(a...  17.6 us
    ppermute x13, starting transfers between devices, swapped(): lax.ppermute(value, axis, [(at, at ^ bit) for at in range(lax.axis_size(a...  9.48 us
    ppermute x2, starting transfers between devices, shifted(): lax.ppermute(value, 'ctx', [(at, at + steps) for at in range(first, last)])  7.97 us
    ppermute x3, starting transfers between devices, rotated(): lax.ppermute(value, 'ctx', [(at, (at + steps) % count) for at in range(co...  7.79 us
    unnamed x10, local copies, waits for them, and re-layouts  3.58 us
    pallas_call x1, Pallas kernels, attention(): pl.pallas_call(kernel, out_shape=(jax.ShapeDtypeStruct((heads, HEAD_SIZE,...  3.36 us
    pallas_call x3, Pallas kernels, level_gradients(): pl.pallas_call(functools.partial(level_kernel, level, p_at), out_shape=(j...  3.19 us
    pallas_call x1, Pallas kernels, near_attention(): pl.pallas_call(near_kernel, out_shape=(jax.ShapeDtypeStruct((depth * LEVE...  2.26 us
  transfers between devices with their start and end apart: 18, of which 8 were waited for; matrix products, arithmetic and copies ran while one was open for 2% of the time, Pallas kernels for 12%

profile of v1, /device:TPU:0, one launch (start us, length us, event | category | flops | bytes accessed | tf_op | source)
XLA Modules:
  0.0 63.0 jit_solution(14253063235455214659)
XLA Ops:
  0.6 1.6 %pack.1.own_hbm = bf16[144,512]{1,0:T(8,128)(2,1)} custom-call(bf16[128,256]{1,0:T(8,128)(2,1)} %bitcast.17, bf16[128,256]{1,0:T(8,128)(2,1)} %bitcast.18, s32[1,128]{1,0:T(1,128)} %docs_hbm.1), custom_call_target="tpu_custom_call" | custom-call | tf_op jit(solution)/shard_map/pack/pallas_call | solution.py:59
  2.2 3.0 %collective-permute-start.1 = (bf16[144,512]{1,0:T(8,128)(2,1)}, bf16[144,512]{1,0:T(8,128)(2,1)S(1)}, u32[]{:S(2)}, u32[]{:S(2)}) collective-permute-start(bf16[144,512]{1,0:T(8,128)(2,1)} %pack.1.own_hbm), channel_id=1, source_target_pairs={{0,2},{1,3},{2,0},{3,1},{4,6},{5,7},{6,4},{7,5},{8,10},{9,11},{10,... | collective-permute-start | bytes 442376 | tf_op jit(solution)/shard_map/ppermute | solution.py:516
  5.2 3.5 %collective-permute-start = (bf16[144,512]{1,0:T(8,128)(2,1)}, bf16[144,512]{1,0:T(8,128)(2,1)S(1)}, u32[]{:S(2)}, u32[]{:S(2)}) collective-permute-start(bf16[144,512]{1,0:T(8,128)(2,1)} %pack.1.own_hbm), channel_id=1, source_target_pairs={{0,4},{1,5},{2,6},{3,7},{4,8},{5,9},{6,10},{7,11},{8,12},{9,13},{1... | collective-permute-start | bytes 442376 | tf_op jit(solution)/shard_map/ppermute | solution.py:507
  8.7 4.5 %collective-permute-start.2 = (bf16[144,512]{1,0:T(8,128)(2,1)}, bf16[144,512]{1,0:T(8,128)(2,1)S(1)}, u32[]{:S(2)}, u32[]{:S(2)}) collective-permute-start(bf16[144,512]{1,0:T(8,128)(2,1)} %pack.1.own_hbm), channel_id=1, source_target_pairs={{0,8},{1,9},{2,10},{3,11},{4,12},{5,13},{6,14},{7,15},{16,24},{17,... | collective-permute-start | bytes 442376 | tf_op jit(solution)/shard_map/ppermute | solution.py:507
  13.2 0.7 %broadcast_in_dim.15.bias_ref = f32[1,1792]{1,0:T(1,128)S(1)} reshape(f32[1792]{0:T(1024)} %param.11) | data formatting | bytes 14336 | tf_op jit(solution)/shard_map/broadcast_in_dim | solution.py:534
  13.9 0.0 copy-start
  13.9 0.9 %copy-done = bf16[144,512]{1,0:T(8,128)(2,1)S(1)} copy-done((bf16[144,512]{1,0:T(8,128)(2,1)S(1)}, bf16[144,512]{1,0:T(8,128)(2,1)}, u32[]{:S(2)}) %copy-start) | copy-done | bytes 147480
  14.8 0.0 copy-start.1
  14.8 1.0 %copy-done.1 = bf16[1,128,1792]{2,1,0:T(8,128)(2,1)S(1)} copy-done((bf16[1,128,1792]{2,1,0:T(8,128)(2,1)S(1)}, bf16[1,128,1792]{2,1,0:T(8,128)(2,1)}, u32[]{:S(2)}) %copy-start.1) | copy-done | bytes 458776
  15.8 0.0 copy-start.2
  15.8 1.0 %copy-done.2 = bf16[1,128,1792]{2,1,0:T(8,128)(2,1)S(1)} copy-done((bf16[1,128,1792]{2,1,0:T(8,128)(2,1)S(1)}, bf16[1,128,1792]{2,1,0:T(8,128)(2,1)}, u32[]{:S(2)}) %copy-start.2) | copy-done | bytes 458776
  16.9 1.0 %prepare.1 = (bf16[2,896,128]{2,1,0:T(8,128)(2,1)S(1)}, bf16[2,128,896]{2,1,0:T(8,128)(2,1)S(1)}, bf16[144,512]{1,0:T(8,128)(2,1)S(1)}) custom-call(bf16[128,1792]{1,0:T(8,128)(2,1)S(1)} %bitcast.15, f32[1,1792]{1,0:T(1,128)S(1)} %broadcast_in_dim.15.bias_ref, bf16[128,1792]{1,0:T(8,128)(2,1)S(1)} %bitcast.16, bf16[144,512]{1,0:T(8,128)(2,1)S(1)} %copy-done), custom_call_target="tpu_custom_call" | custom-call | flops 917504 | bytes 1835008 | tf_op jit(solution)/shard_map/prepare/pallas_call | solution.py:102
  17.9 0.0 collective-permute-done.1
  17.9 0.0 collective-permute-done
  17.9 0.6 collective-permute-start.3
  18.5 0.0 collective-permute-done.2.far_0
  18.5 4.6 %collective-permute-done.3 = bf16[144,512]{1,0:T(8,128)(2,1)S(1)} collective-permute-done((bf16[144,512]{1,0:T(8,128)(2,1)S(1)}, bf16[144,512]{1,0:T(8,128)(2,1)S(1)}, u32[]{:S(2)}, u32[]{:S(2)}) %collective-permute-start.3) | collective-permute-done | bytes 147488 | tf_op jit(solution)/shard_map/ppermute | solution.py:516
  23.2 0.1 collective-permute-start.4
  23.3 0.6 collective-permute-start.5
  23.9 0.2 collective-permute-start.6
  24.0 1.2 %collective-permute-done.4.near_core_ref = bf16[576,512]{1,0:T(8,128)(2,1)S(1)} collective-permute-done((bf16[576,512]{1,0:T(8,128)(2,1)S(1)}, bf16[576,512]{1,0:T(8,128)(2,1)S(1)}, u32[]{:S(2)}, u32[]{:S(2)}) %collective-permute-start.4) | collective-permute-done | bytes 589856 | tf_op jit(solution)/shard_map/ppermute | solution.py:516
  25.2 2.3 %near_attention.1 = (bf16[8,144,512]{2,1,0:T(8,128)(2,1)S(1)}, bf16[2,512,1792]{2,1,0:T(8,128)(2,1)S(1)}, f32[2,16,896]{2,1,0:T(8,128)S(1)}, f32[2,128,896]{2,1,0:T(8,128)S(1)}) custom-call(s32[1]{0:T(128)} %bitcast.rank_ref, bf16[2,896,128]{2,1,0:T(8,128)(2,1)S(1)} %get-tuple-element.50.q_all, ...), custom_call_target="tpu_custom_call" | custom-call | flops 939524096 | bytes 917504 | tf_op jit(solution)/shard_map/near_attention/pallas_call | solution.py:239
  27.5 2.0 %collective-permute-done.5.far_1 = bf16[144,512]{1,0:T(8,128)(2,1)S(1)} collective-permute-done((bf16[144,512]{1,0:T(8,128)(2,1)S(1)}, bf16[144,512]{1,0:T(8,128)(2,1)S(1)}, u32[]{:S(2)}, u32[]{:S(2)}) %collective-permute-start.5) | collective-permute-done | bytes 147488 | tf_op jit(solution)/shard_map/ppermute | solution.py:516
  29.5 0.0 collective-permute-start.7
  29.5 0.0 collective-permute-done.6.far_2
  29.5 1.4 %collective-permute-done.7.far_3 = bf16[144,512]{1,0:T(8,128)(2,1)S(1)} collective-permute-done((bf16[144,512]{1,0:T(8,128)(2,1)S(1)}, bf16[144,512]{1,0:T(8,128)(2,1)S(1)}, u32[]{:S(2)}, u32[]{:S(2)}) %collective-permute-start.7) | collective-permute-done | bytes 147488 | tf_op jit(solution)/shard_map/ppermute | solution.py:516
  30.9 3.4 %attention.1 = (bf16[2,128,896]{2,1,0:T(8,128)(2,1)S(1)}, bf16[2,128,896]{2,1,0:T(8,128)(2,1)S(1)}, bf16[1,512,1792]{2,1,0:T(8,128)(2,1)S(1)}, bf16[3,512,1792]{...) custom-call(s32[1]{0:T(128)} %bitcast.rank_ref, ...), custom_call_target="tpu_custom_call" | custom-call | flops 1879048192 | bytes 1835008 | tf_op jit(solution)/shard_map/attention/pallas_call | solution.py:411
  34.3 1.6 %collective-permute-start.11 = (f32[4,512]{1,0:T(4,128)S(1)}, f32[4,512]{1,0:T(4,128)S(1)}, u32[]{:S(2)}, u32[]{:S(2)}) collective-permute-start(f32[4,512]{1,0:T(4,128)S(1)} %get-tuple-element.87), channel_id=1, source_target_pairs={{0,16},{16,0},{1,17},{17,1},{2,18},{18,2},{3,19},{19,3},{4,20},{20... | collective-permute-start | bytes 24584 | tf_op jit(solution)/shard_map/ppermute | solution.py:516
  35.8 0.7 %level_gradients.3 = (f32[256,512]{1,0:T(8,128)S(1)}, bf16[256,512]{1,0:T(8,128)(2,1)S(1)}) custom-call(s32[1]{0:T(128)} %bitcast.rank_ref, s32[1]{0:T(128)} %get-tuple-element.66.span_ref, bf16[1,512,1792]{2,1,0:T(8,128)(2,1)S(1)} %get-tuple-element.67.p_buf, bf16[3,512,1792]{2,1,0:T(8,128)(2,1)S(1)} %get-tuple-element.81.ds_buf, ...), custom_call_target="tpu_custom_call" | custom-call | flops 29360128 | bytes 229376 | tf_op jit(solution)/shard_map/level_gradients/pallas_call | solution.py:486
  36.6 0.1 collective-permute-start.8
  36.6 0.7 %level_gradients.4 = (f32[256,512]{1,0:T(8,128)S(1)}, bf16[256,512]{1,0:T(8,128)(2,1)S(1)}) custom-call(s32[1]{0:T(128)} %bitcast.rank_ref, s32[1]{0:T(128)} %get-tuple-element.66.span_ref, bf16[2,512,1792]{2,1,0:T(8,128)(2,1)S(1)} %get-tuple-element.61.p_near.p_buf, bf16[3,512,1792]{2,1,0:T(8,128)(2,1)S(1)} %get-tuple-element.81.ds_buf, ...), custom_call_target="tpu_custom_call" | custom-call | flops 29360128 | bytes 229376 | tf_op jit(solution)/shard_map/level_gradients/pallas_call | solution.py:486
  37.4 0.6 collective-permute-done.11
  38.0 0.1 collective-permute-start.12
  38.1 1.8 %level_gradients.5 = (f32[256,512]{1,0:T(8,128)S(1)}, bf16[256,512]{1,0:T(8,128)(2,1)S(1)}) custom-call(s32[1]{0:T(128)} %bitcast.rank_ref, s32[1]{0:T(128)} %get-tuple-element.66.span_ref, bf16[2,512,1792]{2,1,0:T(8,128)(2,1)S(1)} %get-tuple-element.61.p_near.p_buf, bf16[3,512,1792]{2,1,0:T(8,128)(2,1)S(1)} %get-tuple-element.81.ds_buf, ...), custom_call_target="tpu_custom_call" | custom-call | flops 29360128 | bytes 229376 | tf_op jit(solution)/shard_map/level_gradients/pallas_call | solution.py:486
  39.9 0.6 collective-permute-start.9
  40.5 0.0 collective-permute-done.8
  40.5 0.1 convert_add_fusion.2
  40.6 0.0 collective-permute-done.12
  40.6 0.6 collective-permute-start.14
  41.2 0.1 convert_add_fusion
  41.3 1.6 %collective-permute-start.13 = (bf16[128,512]{1,0:T(8,128)(2,1)S(1)}, bf16[128,512]{1,0:T(8,128)(2,1)S(1)}, u32[]{:S(2)}, u32[]{:S(2)}) collective-permute-start(bf16[128,512]{1,0:T(8,128)(2,1)S(1)} %slice.153), channel_id=1, source_target_pairs={{0,2},{1,3},{2,0},{3,1},{4,6},{5,7},{6,4},{7,5},{8,10},{9,11},{10,... | collective-permute-start | bytes 393224 | tf_op jit(solution)/shard_map/ppermute | solution.py:516
  42.9 4.5 %collective-permute-done.14 = bf16[144,512]{1,0:T(8,128)(2,1)S(1)} collective-permute-done((bf16[144,512]{1,0:T(8,128)(2,1)S(1)}, bf16[144,512]{1,0:T(8,128)(2,1)S(1)}, u32[]{:S(2)}, u32[]{:S(2)}) %collective-permute-start.14) | collective-permute-done | bytes 147488 | tf_op jit(solution)/shard_map/ppermute | solution.py:516
  47.5 6.0 %collective-permute-start.15 = (bf16[144,512]{1,0:T(8,128)(2,1)S(1)}, bf16[144,512]{1,0:T(8,128)(2,1)S(1)}, u32[]{:S(2)}, u32[]{:S(2)}) collective-permute-start(bf16[144,512]{1,0:T(8,128)(2,1)S(1)} %pad_maximum_fusion.2), channel_id=1, source_target_pairs={{0,8},{1,9},{2,10},{3,11},{4,12},{5,13},{6,14},{7,15},{8,0},{9,1},... | collective-permute-start | bytes 442376 | tf_op jit(solution)/shard_map/ppermute | solution.py:512
  53.5 0.0 collective-permute-done.13
  53.6 1.8 %collective-permute-start.16 = (bf16[144,512]{1,0:T(8,128)(2,1)S(1)}, bf16[144,512]{1,0:T(8,128)(2,1)S(1)}, u32[]{:S(2)}, u32[]{:S(2)}) collective-permute-start(bf16[144,512]{1,0:T(8,128)(2,1)S(1)} %pad_maximum_fusion.1), channel_id=1, source_target_pairs={{0,12},{1,13},{2,14},{3,15},{4,0},{5,1},{6,2},{7,3},{8,4},{9,5},{1... | collective-permute-start | bytes 442376 | tf_op jit(solution)/shard_map/ppermute | solution.py:512
  55.4 0.0 collective-permute-done.9
  55.4 0.1 convert_add_fusion.1
  55.5 0.6 collective-permute-start.10
  56.1 0.0 collective-permute-start.17
  56.1 1.2 %row_results.1 = (bf16[128,1792]{1,0:T(8,128)(2,1)}, bf16[128,1792]{1,0:T(8,128)(2,1)}) custom-call(bf16[2,128,896]{2,1,0:T(8,128)(2,1)S(1)} %get-tuple-element.74.att_t, bf16[2,128,896]{2,1,0:T(8,128)(2,1)S(1)} %get-tuple-element.75.dq_t), custom_call_target="tpu_custom_call" | custom-call | flops 458752 | bytes 1835008 | tf_op jit(solution)/shard_map/row_results/pallas_call | solution.py:389
  57.3 3.2 %collective-permute-done.10 = bf16[128,512]{1,0:T(8,128)(2,1)S(1)} collective-permute-done((bf16[128,512]{1,0:T(8,128)(2,1)S(1)}, bf16[128,512]{1,0:T(8,128)(2,1)S(1)}, u32[]{:S(2)}, u32[]{:S(2)}) %collective-permute-start.10) | collective-permute-done | bytes 131104 | tf_op jit(solution)/shard_map/ppermute | solution.py:516
  60.5 1.1 %collective-permute-done.17 = f32[4,512]{1,0:T(4,128)S(1)} collective-permute-done((f32[4,512]{1,0:T(4,128)S(1)}, f32[4,512]{1,0:T(4,128)S(1)}, u32[]{:S(2)}, u32[]{:S(2)}) %collective-permute-start.17) | collective-permute-done | bytes 8224 | tf_op jit(solution)/shard_map/ppermute | solution.py:512
  61.6 0.0 collective-permute-done.16
  61.6 0.0 collective-permute-done.15
  61.6 0.6 copy.11
  62.2 0.1 fusion.4
  62.3 0.7 %slice_bitcast_fusion = (bf16[1,128,256]{2,1,0:T(8,128)(2,1)}, bf16[1,128,256]{2,1,0:T(8,128)(2,1)}) fusion(bf16[128,512]{1,0:T(8,128)(2,1)S(1)} %fusion.4), kind=kLoop, calls=%fused_computation.18 | loop fusion | bytes 262144 | tf_op jit(solution)/shard_map/broadcast_in_dim | solution.py:626
  (22 shorter events, 0.3 us)
Async XLA Ops:
  2.2 15.7 %collective-permute-start.1 = (bf16[144,512]{1,0:T(8,128)(2,1)}, bf16[144,512]{1,0:T(8,128)(2,1)S(1)}, u32[]{:S(2)}, u32[]{:S(2)}) collective-permute-start(bf16[144,512]{1,0:T(8,128)(2,1)} %pack.1.own_hbm), channel_id=1, source_target_pairs={{0,2},{1,3},{2,0},{3,1},{4,6},{5,7},{6,4},{7,5},{8,10},{9,11},{10,... | collective-permute-start | bytes 442376 | tf_op jit(solution)/shard_map/ppermute | solution.py:516
  5.2 12.7 %collective-permute-start = (bf16[144,512]{1,0:T(8,128)(2,1)}, bf16[144,512]{1,0:T(8,128)(2,1)S(1)}, u32[]{:S(2)}, u32[]{:S(2)}) collective-permute-start(bf16[144,512]{1,0:T(8,128)(2,1)} %pack.1.own_hbm), channel_id=1, source_target_pairs={{0,4},{1,5},{2,6},{3,7},{4,8},{5,9},{6,10},{7,11},{8,12},{9,13},{1... | collective-permute-start | bytes 442376 | tf_op jit(solution)/shard_map/ppermute | solution.py:507
  8.7 9.8 %collective-permute-start.2 = (bf16[144,512]{1,0:T(8,128)(2,1)}, bf16[144,512]{1,0:T(8,128)(2,1)S(1)}, u32[]{:S(2)}, u32[]{:S(2)}) collective-permute-start(bf16[144,512]{1,0:T(8,128)(2,1)} %pack.1.own_hbm), channel_id=1, source_target_pairs={{0,8},{1,9},{2,10},{3,11},{4,12},{5,13},{6,14},{7,15},{16,24},{17,... | collective-permute-start | bytes 442376 | tf_op jit(solution)/shard_map/ppermute | solution.py:507
  13.9 0.9 %copy-start = (bf16[144,512]{1,0:T(8,128)(2,1)S(1)}, bf16[144,512]{1,0:T(8,128)(2,1)}, u32[]{:S(2)}) copy-start(bf16[144,512]{1,0:T(8,128)(2,1)} %pack.1.own_hbm) | copy-start | bytes 442372
  14.8 1.0 %copy-start.1 = (bf16[1,128,1792]{2,1,0:T(8,128)(2,1)S(1)}, bf16[1,128,1792]{2,1,0:T(8,128)(2,1)}, u32[]{:S(2)}) copy-start(bf16[1,128,1792]{2,1,0:T(8,128)(2,1)} %param.6) | copy-start | bytes 1376260
  15.8 1.0 %copy-start.2 = (bf16[1,128,1792]{2,1,0:T(8,128)(2,1)S(1)}, bf16[1,128,1792]{2,1,0:T(8,128)(2,1)}, u32[]{:S(2)}) copy-start(bf16[1,128,1792]{2,1,0:T(8,128)(2,1)} %param.9) | copy-start | bytes 1376260
  17.9 5.2 %collective-permute-start.3 = (bf16[144,512]{1,0:T(8,128)(2,1)S(1)}, bf16[144,512]{1,0:T(8,128)(2,1)S(1)}, u32[]{:S(2)}, u32[]{:S(2)}) collective-permute-start(bf16[144,512]{1,0:T(8,128)(2,1)S(1)} %collective-permute-done), channel_id=1, source_target_pairs={{0,2},{1,3},{2,0},{3,1},{4,6},{5,7},{6,4},{7,5},{8,10},{9,11},{10,... | collective-permute-start | bytes 442376 | tf_op jit(solution)/shard_map/ppermute | solution.py:516
  23.2 2.1 %collective-permute-start.4 = (bf16[576,512]{1,0:T(8,128)(2,1)S(1)}, bf16[576,512]{1,0:T(8,128)(2,1)S(1)}, u32[]{:S(2)}, u32[]{:S(2)}) collective-permute-start(bf16[576,512]{1,0:T(8,128)(2,1)S(1)} %constant_dynamic-update-slice_fusion.near_ref), channel_id=1, source_target_pairs={{0,1},{1,0},{2,3},{3,2},{4,5},{5,4},{6,7},{7,6},{8,9},{9,8},{10,11... | collective-permute-start | bytes 1769480 | tf_op jit(solution)/shard_map/ppermute | solution.py:516
  23.3 6.3 %collective-permute-start.5 = (bf16[144,512]{1,0:T(8,128)(2,1)S(1)}, bf16[144,512]{1,0:T(8,128)(2,1)S(1)}, u32[]{:S(2)}, u32[]{:S(2)}) collective-permute-start(bf16[144,512]{1,0:T(8,128)(2,1)S(1)} %collective-permute-done.2.far_0), channel_id=1, source_target_pairs={{0,2},{1,3},{2,0},{3,1},{4,6},{5,7},{6,4},{7,5},{8,10},{9,11},{10,... | collective-permute-start | bytes 442376 | tf_op jit(solution)/shard_map/ppermute | solution.py:516
  23.9 5.7 %collective-permute-start.6 = (bf16[144,512]{1,0:T(8,128)(2,1)S(1)}, bf16[144,512]{1,0:T(8,128)(2,1)S(1)}, u32[]{:S(2)}, u32[]{:S(2)}) collective-permute-start(bf16[144,512]{1,0:T(8,128)(2,1)S(1)} %collective-permute-done.2.far_0), channel_id=1, source_target_pairs={{0,1},{1,0},{2,3},{3,2},{4,5},{5,4},{6,7},{7,6},{8,9},{9,8},{10,11... | collective-permute-start | bytes 442376 | tf_op jit(solution)/shard_map/ppermute | solution.py:516
  29.5 1.4 %collective-permute-start.7 = (bf16[144,512]{1,0:T(8,128)(2,1)S(1)}, bf16[144,512]{1,0:T(8,128)(2,1)S(1)}, u32[]{:S(2)}, u32[]{:S(2)}) collective-permute-start(bf16[144,512]{1,0:T(8,128)(2,1)S(1)} %collective-permute-done.5.far_1), channel_id=1, source_target_pairs={{0,1},{1,0},{2,3},{3,2},{4,5},{5,4},{6,7},{7,6},{8,9},{9,8},{10,11... | collective-permute-start | bytes 442376 | tf_op jit(solution)/shard_map/ppermute | solution.py:516
  34.3 3.7 %collective-permute-start.11 = (f32[4,512]{1,0:T(4,128)S(1)}, f32[4,512]{1,0:T(4,128)S(1)}, u32[]{:S(2)}, u32[]{:S(2)}) collective-permute-start(f32[4,512]{1,0:T(4,128)S(1)} %get-tuple-element.87), channel_id=1, source_target_pairs={{0,16},{16,0},{1,17},{17,1},{2,18},{18,2},{3,19},{19,3},{4,20},{20... | collective-permute-start | bytes 24584 | tf_op jit(solution)/shard_map/ppermute | solution.py:516
  36.6 3.9 %collective-permute-start.8 = (bf16[256,512]{1,0:T(8,128)(2,1)S(1)}, bf16[256,512]{1,0:T(8,128)(2,1)S(1)}, u32[]{:S(2)}, u32[]{:S(2)}) collective-permute-start(bf16[256,512]{1,0:T(8,128)(2,1)S(1)} %get-tuple-element.72), channel_id=1, source_target_pairs={{0,1},{1,0},{2,3},{3,2},{4,5},{5,4},{6,7},{7,6},{8,9},{9,8},{10,11... | collective-permute-start | bytes 786440 | tf_op jit(solution)/shard_map/ppermute | solution.py:516
  38.0 2.5 %collective-permute-start.12 = (bf16[272,512]{1,0:T(8,128)(2,1)S(1)}, bf16[272,512]{1,0:T(8,128)(2,1)S(1)}, u32[]{:S(2)}, u32[]{:S(2)}) collective-permute-start(bf16[272,512]{1,0:T(8,128)(2,1)S(1)} %pad_maximum_fusion), channel_id=1, source_target_pairs={{0,1},{1,0},{2,3},{3,2},{4,5},{5,4},{6,7},{7,6},{8,9},{9,8},{10,11... | collective-permute-start | bytes 835592 | tf_op jit(solution)/shard_map/ppermute | solution.py:516
  39.9 15.5 %collective-permute-start.9 = (bf16[256,512]{1,0:T(8,128)(2,1)S(1)}, bf16[256,512]{1,0:T(8,128)(2,1)S(1)}, u32[]{:S(2)}, u32[]{:S(2)}) collective-permute-start(bf16[256,512]{1,0:T(8,128)(2,1)S(1)} %get-tuple-element.84), channel_id=1, source_target_pairs={{0,1},{1,0},{2,3},{3,2},{4,5},{5,4},{6,7},{7,6},{8,9},{9,8},{10,11... | collective-permute-start | bytes 786440 | tf_op jit(solution)/shard_map/ppermute | solution.py:516
  40.6 6.8 %collective-permute-start.14 = (bf16[144,512]{1,0:T(8,128)(2,1)S(1)}, bf16[144,512]{1,0:T(8,128)(2,1)S(1)}, u32[]{:S(2)}, u32[]{:S(2)}) collective-permute-start(bf16[144,512]{1,0:T(8,128)(2,1)S(1)} %pad_maximum_fusion.3), channel_id=1, source_target_pairs={{0,2},{1,3},{2,0},{3,1},{4,6},{5,7},{6,4},{7,5},{8,10},{9,11},{10,... | collective-permute-start | bytes 442376 | tf_op jit(solution)/shard_map/ppermute | solution.py:516
  41.3 12.2 %collective-permute-start.13 = (bf16[128,512]{1,0:T(8,128)(2,1)S(1)}, bf16[128,512]{1,0:T(8,128)(2,1)S(1)}, u32[]{:S(2)}, u32[]{:S(2)}) collective-permute-start(bf16[128,512]{1,0:T(8,128)(2,1)S(1)} %slice.153), channel_id=1, source_target_pairs={{0,2},{1,3},{2,0},{3,1},{4,6},{5,7},{6,4},{7,5},{8,10},{9,11},{10,... | collective-permute-start | bytes 393224 | tf_op jit(solution)/shard_map/ppermute | solution.py:516
  47.5 14.1 %collective-permute-start.15 = (bf16[144,512]{1,0:T(8,128)(2,1)S(1)}, bf16[144,512]{1,0:T(8,128)(2,1)S(1)}, u32[]{:S(2)}, u32[]{:S(2)}) collective-permute-start(bf16[144,512]{1,0:T(8,128)(2,1)S(1)} %pad_maximum_fusion.2), channel_id=1, source_target_pairs={{0,8},{1,9},{2,10},{3,11},{4,12},{5,13},{6,14},{7,15},{8,0},{9,1},... | collective-permute-start | bytes 442376 | tf_op jit(solution)/shard_map/ppermute | solution.py:512
  53.6 8.1 %collective-permute-start.16 = (bf16[144,512]{1,0:T(8,128)(2,1)S(1)}, bf16[144,512]{1,0:T(8,128)(2,1)S(1)}, u32[]{:S(2)}, u32[]{:S(2)}) collective-permute-start(bf16[144,512]{1,0:T(8,128)(2,1)S(1)} %pad_maximum_fusion.1), channel_id=1, source_target_pairs={{0,12},{1,13},{2,14},{3,15},{4,0},{5,1},{6,2},{7,3},{8,4},{9,5},{1... | collective-permute-start | bytes 442376 | tf_op jit(solution)/shard_map/ppermute | solution.py:512
  55.5 5.0 %collective-permute-start.10 = (bf16[128,512]{1,0:T(8,128)(2,1)S(1)}, bf16[128,512]{1,0:T(8,128)(2,1)S(1)}, u32[]{:S(2)}, u32[]{:S(2)}) collective-permute-start(bf16[128,512]{1,0:T(8,128)(2,1)S(1)} %slice.154), channel_id=1, source_target_pairs={{0,2},{1,3},{2,0},{3,1},{4,6},{5,7},{6,4},{7,5},{8,10},{9,11},{10,... | collective-permute-start | bytes 393224 | tf_op jit(solution)/shard_map/ppermute | solution.py:516
  56.1 5.6 %collective-permute-start.17 = (f32[4,512]{1,0:T(4,128)S(1)}, f32[4,512]{1,0:T(4,128)S(1)}, u32[]{:S(2)}, u32[]{:S(2)}) collective-permute-start(f32[4,512]{1,0:T(4,128)S(1)} %get-tuple-element.92), channel_id=1, source_target_pairs={{0,4},{1,5},{2,6},{3,7},{4,8},{5,9},{6,10},{7,11},{8,12},{9,13},{1... | collective-permute-start | bytes 24584 | tf_op jit(solution)/shard_map/ppermute | solution.py:512
